TPU v7x, 256 devices: a whole 4x4x8 slice. The times are simulated.
256 devices in a mesh: grp: 4 (over z_hi, core), vocab: 64 (over x, z_lo, y).
Axes of the slice: x: 4, y: 4, z: 8 (z_hi: 2, z_lo: 4; z = z_hi * 4 + z_lo), core: 2. Of those that a mesh axis runs over, the one named last changes fastest.
Arguments:
- teacher_hidden: bfloat16 [512, 8192], P('vocab', 'grp'), may hold values from -60 to 60
- norm_gain: float32 [8192], P('grp'), may hold values from 0.1 to 1.9
- teacher_weight: bfloat16 [8192, 81920], P('grp', 'vocab'), may hold values from -0.49718446 to 0.49718446
- student_hidden: bfloat16 [512, 3584], P('vocab', 'grp'), may hold values from -4 to 4
- student_weight: bfloat16 [3584, 81920], P('grp', 'vocab'), may hold values from -0.75167224 to 0.75167224
Outputs:
- kl_rows: float32 [512], P('grp')
- hidden_grad: float32 [512, 3584], P('vocab', 'grp')
All inputs are finite; a program needn't handle non-finite values.
Results may differ from a plain program's by a relative error of at most 0.0071.
Values may be sent and summed in bfloat16 or wider, within the bound.
No kernel may reach another device: no remote copies, remote signals or barrier semaphores. Data moves between devices by JAX's collectives and lax.ppermute only.
A program may use at most 64 MiB of HBM per device.

v0:
```python
import jax
import jax.numpy as jnp
from jax import lax
from jax.sharding import Mesh, PartitionSpec as P

D_T = 8192
EPS = 1e-06
GRP = ("zh", "c")
VOC = ("x", "zl", "y")
SIZE = {"zh": 2, "c": 2, "x": 4, "zl": 4, "y": 4}
GRAD_SCALE = 2.0**15


def shift(value, axis, distance):
    n = SIZE[axis]
    return lax.ppermute(value, axis, [(i, (i + distance) % n) for i in range(n)])


def gather4(value, axis, place):
    me = lax.axis_index(axis)
    came = {d: shift(value, axis, d) for d in (2, 1, 3)}
    blocks = [jnp.expand_dims(b, place) for b in (value, came[1], came[2], came[3])]
    shape = value.shape[:place] + (4,) + value.shape[place:]
    out = jnp.zeros(shape, value.dtype)
    for d in range(4):
        start = [0] * len(shape)
        start[place] = (me + 4 - d) % 4
        out = lax.dynamic_update_slice(out, blocks[d], start)
    return out


def gather_hidden(value, cut):
    value = gather4(value, "zl", 0)
    first, second = value[..., :cut], value[..., cut:]
    first = gather4(gather4(first, "y", 1), "x", 0)
    second = gather4(gather4(second, "x", 0), "y", 2)
    return first.reshape(512, -1), second.reshape(512, -1)


def scatter_pair(value, axis):
    me = lax.axis_index(axis)
    give = lax.dynamic_index_in_dim(value, 1 - me, 0, keepdims=False).astype(jnp.float16)
    keep = lax.dynamic_index_in_dim(value, me, 0, keepdims=False)
    return keep + shift(give, axis, 1).astype(jnp.float32)


def logits_of(hidden, weight):
    terms = jnp.dot(hidden, weight, preferred_element_type=jnp.float32)
    terms = terms.reshape(2, 2, 128, 1280).transpose(1, 0, 2, 3)
    return scatter_pair(scatter_pair(terms, "c"), "zh")


def pick(value, index, dim):
    return lax.dynamic_index_in_dim(value, index, dim, keepdims=False)


def grad_terms(mine, other, weight):
    def terms(grad):
        value = lax.dot_general(grad, weight, (((1,), (1,)), ((), ())), preferred_element_type=jnp.float32)
        return (value * GRAD_SCALE).astype(jnp.float16)

    return terms(mine), terms(other)


def in_order(mine, other, place):
    return jnp.where(place == 0, mine, other), jnp.where(place == 0, other, mine)


def scatter_grad(near, far):
    zh, c, zl = lax.axis_index("zh"), lax.axis_index("c"), lax.axis_index("zl")
    near, far = in_order(*near, c), in_order(*far, c)
    even, odd = in_order(near[0], far[0], zh), in_order(near[1], far[1], zh)
    terms = jnp.stack([even[0], odd[0], even[1], odd[1]])
    terms = terms.reshape(4, 4, 4, 8, 896).transpose(0, 2, 1, 3, 4)
    parts = lax.all_to_all(terms.reshape(16, 32, 896), ("x", "y"), 0, 0, tiled=True)
    total = jnp.sum(parts.astype(jnp.float32), axis=0).reshape(4, 8, 896)
    half = total.astype(jnp.float16)
    mine = pick(total, zl, 0)
    for d in (1, 2, 3):
        mine = mine + shift(pick(half, (zl + d) % 4, 0), "zl", d).astype(jnp.float32)
    return mine * (1.0 / GRAD_SCALE)


def merge(stats):
    padded = jnp.concatenate([stats, jnp.zeros((3, 128), jnp.float32)])
    every = lax.all_to_all(jnp.tile(padded, (64, 1)), VOC, 0, 0, tiled=True).reshape(64, 8, 128)
    t_top = jnp.max(every[:, 0], axis=0)
    s_top = jnp.max(every[:, 3], axis=0)
    t_scale = jnp.exp(every[:, 0] - t_top)
    s_scale = jnp.exp(every[:, 3] - s_top)
    t_total = jnp.sum(every[:, 1] * t_scale, axis=0)
    cross = jnp.sum(every[:, 2] * t_scale, axis=0)
    s_total = jnp.sum(every[:, 4] * s_scale, axis=0)
    return t_top + jnp.log(t_total), s_top + jnp.log(s_total), cross / t_total


def on_device(teacher_hidden, norm_gain, teacher_weight, student_hidden, student_weight):
    cut = 1536
    own = jnp.pad(teacher_hidden, ((0, 0), (0, 896))) + jnp.pad(student_hidden, ((0, 0), (2048, 0)))
    first, second = gather_hidden(own, cut)
    left = 2048 - cut
    wide = jnp.concatenate([first, second[:, :left]], axis=1).astype(jnp.float32)
    squares = jnp.sum(wide * wide, axis=1)
    squares = squares + shift(squares, "c", 1)
    squares = squares + shift(squares, "zh", 1)
    student = logits_of(second[:, left:], student_weight)
    inverse = lax.rsqrt(squares / D_T + EPS)
    normed = (wide * inverse[:, None] * norm_gain[None, :]).astype(jnp.bfloat16)
    teacher = logits_of(normed, teacher_weight)

    t_top = jnp.max(teacher, axis=1)
    s_top = jnp.max(student, axis=1)
    t_exp = jnp.exp(teacher - t_top[:, None])
    stats = jnp.stack(
        [
            t_top,
            jnp.sum(t_exp, axis=1),
            jnp.sum(t_exp * (teacher - student), axis=1),
            s_top,
            jnp.sum(jnp.exp(student - s_top[:, None]), axis=1),
        ]
    )
    t_log, s_log, cross = merge(stats)
    kl_rows = cross - t_log + s_log
    grad = jnp.exp(student - s_log[:, None]) - jnp.exp(teacher - t_log[:, None])
    grad = grad.astype(jnp.bfloat16)

    near = grad_terms(grad, shift(grad, "c", 1), student_weight)
    far, near = lax.optimization_barrier((shift(grad, "zh", 1), near))
    far = grad_terms(far, shift(far, "c", 1), student_weight)
    return kl_rows, scatter_grad(near, far)


def solution(mesh):
    fine = Mesh(mesh.devices.reshape(2, 2, 4, 4, 4), GRP + VOC)
    placed = (P(VOC, GRP), P(GRP), P(GRP, VOC), P(VOC, GRP), P(GRP, VOC))
    return jax.shard_map(
        on_device,
        mesh=fine,
        in_specs=placed,
        out_specs=(P(GRP), P(VOC, GRP)),
        check_vma=False,
    )
```

profile of v0, /device:TPU:8, one launch (start us, length us, event | category | flops | bytes accessed | tf_op | source)
XLA Modules:
  0.0 171.1 jit_solution(2981524079082259594)
XLA Ops:
  0.6 0.9 pad_add_fusion
  1.6 1.9 %collective-permute-start = (bf16[8,2944]{1,0:T(8,128)(2,1)S(1)}, bf16[8,2944]{1,0:T(8,128)(2,1)S(1)}, u32[]{:S(2)}, u32[]{:S(2)}) collective-permute-start(bf16[8,2944]{1,0:T(8,128)(2,1)S(1)} %pad_add_fusion), channel_id=1, source_target_pairs={{0,4},{4,8},{8,12},{12,0},{1,5},{5,9},{9,13},{13,1},{2,6},{6,10},{... | collective-permute-start | bytes 141320 | tf_op jit(solution)/shard_map/ppermute | solution.py:16
  3.5 3.3 %collective-permute-start.1 = (bf16[8,2944]{1,0:T(8,128)(2,1)S(1)}, bf16[8,2944]{1,0:T(8,128)(2,1)S(1)}, u32[]{:S(2)}, u32[]{:S(2)}) collective-permute-start(bf16[8,2944]{1,0:T(8,128)(2,1)S(1)} %pad_add_fusion), channel_id=1, source_target_pairs={{0,8},{4,12},{8,0},{12,4},{1,9},{5,13},{9,1},{13,5},{2,10},{6,14},... | collective-permute-start | bytes 141320 | tf_op jit(solution)/shard_map/ppermute | solution.py:16
  6.8 1.0 collective-permute-start.2
  7.8 0.8 bitcast_dynamic-update-slice_fusion.19
  8.6 1.7 collective-permute-done.1
  10.3 0.5 collective-permute-done.2
  10.9 1.6 collective-permute-start.9
  12.4 2.7 %collective-permute-start.10 = (bf16[4,8,1408]{2,1,0:T(8,128)(2,1)S(1)}, bf16[4,8,1408]{2,1,0:T(8,128)(2,1)S(1)}, u32[]{:S(2)}, u32[]{:S(2)}) collective-permute-start(bf16[4,8,1408]{2,1,0:T(8,128)(2,1)S(1)} %slice.39), channel_id=1, source_target_pairs={{0,32},{16,48},{32,0},{48,16},{1,33},{17,49},{33,1},{49,17},{2,34}... | collective-permute-start | bytes 270344 | tf_op jit(solution)/shard_map/ppermute | solution.py:16
  15.2 1.4 collective-permute-start.11
  16.6 1.6 collective-permute-start.3
  18.2 0.9 collective-permute-start.4
  19.3 2.5 %collective-permute-start.5 = (bf16[4,8,1536]{2,1,0:T(8,128)(2,1)S(1)}, bf16[4,8,1536]{2,1,0:T(8,128)(2,1)S(1)}, u32[]{:S(2)}, u32[]{:S(2)}) collective-permute-start(bf16[4,8,1536]{2,1,0:T(8,128)(2,1)S(1)} %slice.38), channel_id=1, source_target_pairs={{0,3},{1,0},{2,1},{3,2},{4,7},{5,4},{6,5},{7,6},{8,11},{9,8},{10,9... | collective-permute-start | bytes 294920 | tf_op jit(solution)/shard_map/ppermute | solution.py:16
  22.0 3.4 %collective-permute-start.13 = (bf16[4,4,8,1408]{3,2,1,0:T(8,128)(2,1)S(1)}, bf16[4,4,8,1408]{3,2,1,0:T(8,128)(2,1)S(1)}, u32[]{:S(2)}, u32[]{:S(2)}) collective-permute-start(bf16[4,4,8,1408]{3,2,1,0:T(8,128)(2,1)S(1)} %bitcast_dynamic-update-slice_fusion.12), channel_id=1, source_target_pairs={{0,2},{1,3},{2,0},{3,1},{4,6},{5,7},{6,4},{7,5},{8,10},{9,11},{10,... | collective-permute-start | bytes 1081352 | tf_op jit(solution)/shard_map/ppermute | solution.py:16
  25.4 0.1 broadcast_in_dim.101
  25.7 5.7 %collective-permute-done.5 = bf16[4,8,1536]{2,1,0:T(8,128)(2,1)S(1)} collective-permute-done((bf16[4,8,1536]{2,1,0:T(8,128)(2,1)S(1)}, bf16[4,8,1536]{2,1,0:T(8,128)(2,1)S(1)}, u32[]{:S(2)}, u32[]{:S(2)}) %collective-permute-start.5) | collective-permute-done | bytes 98336 | tf_op jit(solution)/shard_map/ppermute | solution.py:16
  31.4 0.7 collective-permute-start.6
  32.1 0.1 broadcast_in_dim.86
  32.3 1.0 collective-permute-done.12
  33.3 1.8 %collective-permute-start.8 = (bf16[4,4,8,1536]{3,2,1,0:T(8,128)(2,1)S(1)}, bf16[4,4,8,1536]{3,2,1,0:T(8,128)(2,1)S(1)}, u32[]{:S(2)}, u32[]{:S(2)}) collective-permute-start(bf16[4,4,8,1536]{3,2,1,0:T(8,128)(2,1)S(1)} %bitcast_dynamic-update-slice_fusion.11), channel_id=1, source_target_pairs={{0,48},{16,0},{32,16},{48,32},{1,49},{17,1},{33,17},{49,33},{2,50}... | collective-permute-start | bytes 1179656 | tf_op jit(solution)/shard_map/ppermute | solution.py:16
  35.3 5.2 %collective-permute-done.14 = bf16[4,4,8,1408]{3,2,1,0:T(8,128)(2,1)S(1)} collective-permute-done((bf16[4,4,8,1408]{3,2,1,0:T(8,128)(2,1)S(1)}, bf16[4,4,8,1408]{3,2,1,0:T(8,128)(2,1)S(1)}, u32[]{:S(2)}, u32[]{:S(2)}) %collective-permute-start.14) | collective-permute-done | bytes 360480 | tf_op jit(solution)/shard_map/ppermute | solution.py:16
  40.6 4.8 %collective-permute-done.6 = bf16[4,4,8,1536]{3,2,1,0:T(8,128)(2,1)S(1)} collective-permute-done((bf16[4,4,8,1536]{3,2,1,0:T(8,128)(2,1)S(1)}, bf16[4,4,8,1536]{3,2,1,0:T(8,128)(2,1)S(1)}, u32[]{:S(2)}, u32[]{:S(2)}) %collective-permute-start.6) | collective-permute-done | bytes 393248 | tf_op jit(solution)/shard_map/ppermute | solution.py:16
  45.4 0.1 collective-permute-done.8
  45.6 0.5 fusion
  46.1 0.3 collective-permute-start.15
  46.4 1.5 fusion.11
  48.0 6.1 %collective-permute-start.16 = (f32[512]{0:T(512)S(1)}, f32[512]{0:T(512)S(1)}, u32[]{:S(2)}, u32[]{:S(2)}) collective-permute-start(f32[512]{0:T(512)S(1)} %add.259), channel_id=1, source_target_pairs={{0,128},{128,0},{1,129},{129,1},{2,130},{130,2},{3,131},{131,3},{4... | collective-permute-start | bytes 6152 | tf_op jit(solution)/shard_map/ppermute | solution.py:16
  54.2 0.3 collective-permute-start.19
  54.5 1.2 collective-permute-done.16
  55.7 3.0 %fusion.3 = f32[512,1280]{1,0:T(8,128)S(1)} fusion(bf16[2048,1280]{1,0:T(8,128)(2,1)S(1)} %bitcast.168, f32[2048]{0:T(1024)S(1)} %copy-done.4, f32[512]{0:T(512)S(1)} %add_rsqrt_fusion, bf16[512,512]{1,0:T(8,128)(2,1)S(1)} %slice.40, bf16[512,1536]{1,0:T(8,128)(2,1)S(1)} %bitcast.142), kind=kOutput, calls=%fused_computation.5 | convolution fusion | flops 2691694592 | bytes 9971712 | tf_op jit(solution)/shard_map/dot_general | solution.py:48
  58.8 0.1 collective-permute-start.17
  58.9 0.1 bitcast_add_fusion
  59.1 6.0 %collective-permute-start.20 = (f16[128,1280]{1,0:T(8,128)(2,1)S(1)}, f16[128,1280]{1,0:T(8,128)(2,1)S(1)}, u32[]{:S(2)}, u32[]{:S(2)}) collective-permute-start(f16[128,1280]{1,0:T(8,128)(2,1)S(1)} %fusion.17), channel_id=1, source_target_pairs={{0,128},{128,0},{1,129},{129,1},{2,130},{130,2},{3,131},{131,3},{4... | collective-permute-start | bytes 983048 | tf_op jit(solution)/shard_map/ppermute | solution.py:16
  65.1 0.2 bitcast_add_fusion.1
  65.4 0.9 fusion.16
  66.2 0.3 copy-done.3
  66.6 1.8 %collective-permute-start.18 = (f16[128,1280]{1,0:T(8,128)(2,1)}, f16[128,1280]{1,0:T(8,128)(2,1)S(1)}, u32[]{:S(2)}, u32[]{:S(2)}) collective-permute-start(f16[128,1280]{1,0:T(8,128)(2,1)} %fusion.16), channel_id=1, source_target_pairs={{0,128},{128,0},{1,129},{129,1},{2,130},{130,2},{3,131},{131,3},{4... | collective-permute-start | bytes 983048 | tf_op jit(solution)/shard_map/ppermute | solution.py:16
  68.3 15.5 %collective-permute-done.20 = f16[128,1280]{1,0:T(8,128)(2,1)S(1)} collective-permute-done((f16[128,1280]{1,0:T(8,128)(2,1)S(1)}, f16[128,1280]{1,0:T(8,128)(2,1)S(1)}, u32[]{:S(2)}, u32[]{:S(2)}) %collective-permute-start.20) | collective-permute-done | bytes 327712 | tf_op jit(solution)/shard_map/ppermute | solution.py:16
  83.9 1.2 fusion.23
  85.1 9.6 %collective-permute-done.18 = f16[128,1280]{1,0:T(8,128)(2,1)S(1)} collective-permute-done((f16[128,1280]{1,0:T(8,128)(2,1)}, f16[128,1280]{1,0:T(8,128)(2,1)S(1)}, u32[]{:S(2)}, u32[]{:S(2)}) %collective-permute-start.18) | collective-permute-done | bytes 327712 | tf_op jit(solution)/shard_map/ppermute | solution.py:16
  94.7 1.2 fusion.22
  95.9 1.5 multiply_reduce_fusion
  97.5 19.8 %all_to_all.11 = f32[64,8,128]{2,1,0:T(8,128)S(1)} all-to-all(f32[64,8,128]{2,1,0:T(8,128)S(1)} %tile.2), channel_id=1, replica_groups=mesh['zh'=2,'c'=2,'x'=4,'zl'=4,'y'=4] {'x','zl','y'}, dimensions={0} | all-to-all | bytes 524288 | tf_op jit(solution)/shard_map/all_to_all | solution.py:86
  117.3 0.1 fusion.24
  117.5 0.5 subtract_add_fusion
  118.0 1.6 subtract_convert_fusion
  119.6 0.1 collective-permute-start.22
  119.7 4.7 %collective-permute-start.21 = (bf16[128,1280]{1,0:T(8,128)(2,1)S(1)}, bf16[128,1280]{1,0:T(8,128)(2,1)S(1)}, u32[]{:S(2)}, u32[]{:S(2)}) collective-permute-start(bf16[128,1280]{1,0:T(8,128)(2,1)S(1)} %subtract_convert_fusion), channel_id=1, source_target_pairs={{0,128},{128,0},{1,129},{129,1},{2,130},{130,2},{3,131},{131,3},{4... | collective-permute-start | bytes 983048 | tf_op jit(solution)/shard_map/ppermute | solution.py:16
  124.4 0.9 fusion.7
  125.3 0.9 fusion.8
  126.2 14.7 %collective-permute-done.21 = bf16[128,1280]{1,0:T(8,128)(2,1)S(1)} collective-permute-done((bf16[128,1280]{1,0:T(8,128)(2,1)S(1)}, bf16[128,1280]{1,0:T(8,128)(2,1)S(1)}, u32[]{:S(2)}, u32[]{:S(2)}) %collective-permute-start.21) | collective-permute-done | bytes 327712 | tf_op jit(solution)/shard_map/ppermute | solution.py:16
  140.9 0.8 fusion.9
  141.7 0.8 collective-permute-done.23
  142.5 0.9 fusion.10
  143.4 0.3 broadcast_select_fusion.7
  143.6 0.3 pad_maximum_fusion.2
  143.9 0.2 copy.50
  144.1 18.5 %all_to_all.12 = f16[16,32,896]{2,1,0:T(8,128)(2,1)S(1)} all-to-all(f16[16,32,896]{2,1,0:T(8,128)(2,1)S(1)} %bitcast.143), channel_id=1, replica_groups=mesh['zh'=2,'c'=2,'x'=4,'zl'=4,'y'=4] {'x','y'}, dimensions={0} | all-to-all | bytes 1835008 | tf_op jit(solution)/shard_map/all_to_all | solution.py:75
  162.7 0.1 convert_reduce_fusion
  162.9 2.1 %collective-permute-start.25 = (f16[8,896]{1,0:T(8,128)(2,1)S(1)}, f16[8,896]{1,0:T(8,128)(2,1)S(1)}, u32[]{:S(2)}, u32[]{:S(2)}) collective-permute-start(f16[8,896]{1,0:T(8,128)(2,1)S(1)} %get-tuple-element.27), channel_id=1, source_target_pairs={{0,8},{4,12},{8,0},{12,4},{1,9},{5,13},{9,1},{13,5},{2,10},{6,14},... | collective-permute-start | bytes 43016 | tf_op jit(solution)/shard_map/ppermute | solution.py:16
  165.0 1.6 collective-permute-done.26
  166.6 1.0 collective-permute-done.25
  167.6 2.9 %collective-permute-done.24 = f16[8,896]{1,0:T(8,128)(2,1)S(1)} collective-permute-done((f16[8,896]{1,0:T(8,128)(2,1)S(1)}, f16[8,896]{1,0:T(8,128)(2,1)S(1)}, u32[]{:S(2)}, u32[]{:S(2)}) %collective-permute-start.24) | collective-permute-done | bytes 14368 | tf_op jit(solution)/shard_map/ppermute | solution.py:16
  170.5 0.6 fusion.20
  (70 shorter events, 1.3 us)
Async XLA Ops:
  0.6 45.8 %copy-start = (bf16[896,1280]{1,0:T(8,128)(2,1)S(1)}, bf16[896,1280]{1,0:T(8,128)(2,1)}, u32[]{:S(2)}) copy-start(bf16[896,1280]{1,0:T(8,128)(2,1)} %param.9) | copy-start | bytes 6881284
  1.6 7.0 %collective-permute-start = (bf16[8,2944]{1,0:T(8,128)(2,1)S(1)}, bf16[8,2944]{1,0:T(8,128)(2,1)S(1)}, u32[]{:S(2)}, u32[]{:S(2)}) collective-permute-start(bf16[8,2944]{1,0:T(8,128)(2,1)S(1)} %pad_add_fusion), channel_id=1, source_target_pairs={{0,4},{4,8},{8,12},{12,0},{1,5},{5,9},{9,13},{13,1},{2,6},{6,10},{... | collective-permute-start | bytes 141320 | tf_op jit(solution)/shard_map/ppermute | solution.py:16
  3.5 6.8 %collective-permute-start.1 = (bf16[8,2944]{1,0:T(8,128)(2,1)S(1)}, bf16[8,2944]{1,0:T(8,128)(2,1)S(1)}, u32[]{:S(2)}, u32[]{:S(2)}) collective-permute-start(bf16[8,2944]{1,0:T(8,128)(2,1)S(1)} %pad_add_fusion), channel_id=1, source_target_pairs={{0,8},{4,12},{8,0},{12,4},{1,9},{5,13},{9,1},{13,5},{2,10},{6,14},... | collective-permute-start | bytes 141320 | tf_op jit(solution)/shard_map/ppermute | solution.py:16
  6.8 4.1 %collective-permute-start.2 = (bf16[8,2944]{1,0:T(8,128)(2,1)S(1)}, bf16[8,2944]{1,0:T(8,128)(2,1)S(1)}, u32[]{:S(2)}, u32[]{:S(2)}) collective-permute-start(bf16[8,2944]{1,0:T(8,128)(2,1)S(1)} %pad_add_fusion), channel_id=1, source_target_pairs={{0,12},{4,0},{8,4},{12,8},{1,13},{5,1},{9,5},{13,9},{2,14},{6,2},{... | collective-permute-start | bytes 141320 | tf_op jit(solution)/shard_map/ppermute | solution.py:16
  10.9 8.4 %collective-permute-start.9 = (bf16[4,8,1408]{2,1,0:T(8,128)(2,1)S(1)}, bf16[4,8,1408]{2,1,0:T(8,128)(2,1)S(1)}, u32[]{:S(2)}, u32[]{:S(2)}) collective-permute-start(bf16[4,8,1408]{2,1,0:T(8,128)(2,1)S(1)} %slice.39), channel_id=1, source_target_pairs={{0,16},{16,32},{32,48},{48,0},{1,17},{17,33},{33,49},{49,1},{2,18}... | collective-permute-start | bytes 270344 | tf_op jit(solution)/shard_map/ppermute | solution.py:16
  12.4 9.4 %collective-permute-start.10 = (bf16[4,8,1408]{2,1,0:T(8,128)(2,1)S(1)}, bf16[4,8,1408]{2,1,0:T(8,128)(2,1)S(1)}, u32[]{:S(2)}, u32[]{:S(2)}) collective-permute-start(bf16[4,8,1408]{2,1,0:T(8,128)(2,1)S(1)} %slice.39), channel_id=1, source_target_pairs={{0,32},{16,48},{32,0},{48,16},{1,33},{17,49},{33,1},{49,17},{2,34}... | collective-permute-start | bytes 270344 | tf_op jit(solution)/shard_map/ppermute | solution.py:16
  15.2 6.7 %collective-permute-start.11 = (bf16[4,8,1408]{2,1,0:T(8,128)(2,1)S(1)}, bf16[4,8,1408]{2,1,0:T(8,128)(2,1)S(1)}, u32[]{:S(2)}, u32[]{:S(2)}) collective-permute-start(bf16[4,8,1408]{2,1,0:T(8,128)(2,1)S(1)} %slice.39), channel_id=1, source_target_pairs={{0,48},{16,0},{32,16},{48,32},{1,49},{17,1},{33,17},{49,33},{2,50}... | collective-permute-start | bytes 270344 | tf_op jit(solution)/shard_map/ppermute | solution.py:16
  16.6 9.0 %collective-permute-start.3 = (bf16[4,8,1536]{2,1,0:T(8,128)(2,1)S(1)}, bf16[4,8,1536]{2,1,0:T(8,128)(2,1)S(1)}, u32[]{:S(2)}, u32[]{:S(2)}) collective-permute-start(bf16[4,8,1536]{2,1,0:T(8,128)(2,1)S(1)} %slice.38), channel_id=1, source_target_pairs={{0,1},{1,2},{2,3},{3,0},{4,5},{5,6},{6,7},{7,4},{8,9},{9,10},{10,1... | collective-permute-start | bytes 294920 | tf_op jit(solution)/shard_map/ppermute | solution.py:16
  18.2 7.4 %collective-permute-start.4 = (bf16[4,8,1536]{2,1,0:T(8,128)(2,1)S(1)}, bf16[4,8,1536]{2,1,0:T(8,128)(2,1)S(1)}, u32[]{:S(2)}, u32[]{:S(2)}) collective-permute-start(bf16[4,8,1536]{2,1,0:T(8,128)(2,1)S(1)} %slice.38), channel_id=1, source_target_pairs={{0,2},{1,3},{2,0},{3,1},{4,6},{5,7},{6,4},{7,5},{8,10},{9,11},{10,... | collective-permute-start | bytes 294920 | tf_op jit(solution)/shard_map/ppermute | solution.py:16
  19.3 12.1 %collective-permute-start.5 = (bf16[4,8,1536]{2,1,0:T(8,128)(2,1)S(1)}, bf16[4,8,1536]{2,1,0:T(8,128)(2,1)S(1)}, u32[]{:S(2)}, u32[]{:S(2)}) collective-permute-start(bf16[4,8,1536]{2,1,0:T(8,128)(2,1)S(1)} %slice.38), channel_id=1, source_target_pairs={{0,3},{1,0},{2,1},{3,2},{4,7},{5,4},{6,5},{7,6},{8,11},{9,8},{10,9... | collective-permute-start | bytes 294920 | tf_op jit(solution)/shard_map/ppermute | solution.py:16
  21.9 11.4 %collective-permute-start.12 = (bf16[4,4,8,1408]{3,2,1,0:T(8,128)(2,1)S(1)}, bf16[4,4,8,1408]{3,2,1,0:T(8,128)(2,1)S(1)}, u32[]{:S(2)}, u32[]{:S(2)}) collective-permute-start(bf16[4,4,8,1408]{3,2,1,0:T(8,128)(2,1)S(1)} %bitcast_dynamic-update-slice_fusion.12), channel_id=1, source_target_pairs={{0,1},{1,2},{2,3},{3,0},{4,5},{5,6},{6,7},{7,4},{8,9},{9,10},{10,1... | collective-permute-start | bytes 1081352 | tf_op jit(solution)/shard_map/ppermute | solution.py:16
  22.0 13.3 %collective-permute-start.13 = (bf16[4,4,8,1408]{3,2,1,0:T(8,128)(2,1)S(1)}, bf16[4,4,8,1408]{3,2,1,0:T(8,128)(2,1)S(1)}, u32[]{:S(2)}, u32[]{:S(2)}) collective-permute-start(bf16[4,4,8,1408]{3,2,1,0:T(8,128)(2,1)S(1)} %bitcast_dynamic-update-slice_fusion.12), channel_id=1, source_target_pairs={{0,2},{1,3},{2,0},{3,1},{4,6},{5,7},{6,4},{7,5},{8,10},{9,11},{10,... | collective-permute-start | bytes 1081352 | tf_op jit(solution)/shard_map/ppermute | solution.py:16
  25.6 14.9 %collective-permute-start.14 = (bf16[4,4,8,1408]{3,2,1,0:T(8,128)(2,1)S(1)}, bf16[4,4,8,1408]{3,2,1,0:T(8,128)(2,1)S(1)}, u32[]{:S(2)}, u32[]{:S(2)}) collective-permute-start(bf16[4,4,8,1408]{3,2,1,0:T(8,128)(2,1)S(1)} %bitcast_dynamic-update-slice_fusion.12), channel_id=1, source_target_pairs={{0,3},{1,0},{2,1},{3,2},{4,7},{5,4},{6,5},{7,6},{8,11},{9,8},{10,9... | collective-permute-start | bytes 1081352 | tf_op jit(solution)/shard_map/ppermute | solution.py:16
  31.4 14.0 %collective-permute-start.6 = (bf16[4,4,8,1536]{3,2,1,0:T(8,128)(2,1)S(1)}, bf16[4,4,8,1536]{3,2,1,0:T(8,128)(2,1)S(1)}, u32[]{:S(2)}, u32[]{:S(2)}) collective-permute-start(bf16[4,4,8,1536]{3,2,1,0:T(8,128)(2,1)S(1)} %bitcast_dynamic-update-slice_fusion.11), channel_id=1, source_target_pairs={{0,16},{16,32},{32,48},{48,0},{1,17},{17,33},{33,49},{49,1},{2,18}... | collective-permute-start | bytes 1179656 | tf_op jit(solution)/shard_map/ppermute | solution.py:16
  32.1 13.3 %collective-permute-start.7 = (bf16[4,4,8,1536]{3,2,1,0:T(8,128)(2,1)S(1)}, bf16[4,4,8,1536]{3,2,1,0:T(8,128)(2,1)S(1)}, u32[]{:S(2)}, u32[]{:S(2)}) collective-permute-start(bf16[4,4,8,1536]{3,2,1,0:T(8,128)(2,1)S(1)} %bitcast_dynamic-update-slice_fusion.11), channel_id=1, source_target_pairs={{0,32},{16,48},{32,0},{48,16},{1,33},{17,49},{33,1},{49,17},{2,34}... | collective-permute-start | bytes 1179656 | tf_op jit(solution)/shard_map/ppermute | solution.py:16
  33.3 12.3 %collective-permute-start.8 = (bf16[4,4,8,1536]{3,2,1,0:T(8,128)(2,1)S(1)}, bf16[4,4,8,1536]{3,2,1,0:T(8,128)(2,1)S(1)}, u32[]{:S(2)}, u32[]{:S(2)}) collective-permute-start(bf16[4,4,8,1536]{3,2,1,0:T(8,128)(2,1)S(1)} %bitcast_dynamic-update-slice_fusion.11), channel_id=1, source_target_pairs={{0,48},{16,0},{32,16},{48,32},{1,49},{17,1},{33,17},{49,33},{2,50}... | collective-permute-start | bytes 1179656 | tf_op jit(solution)/shard_map/ppermute | solution.py:16
  45.6 10.1 %slice-start = ((s8[5242880]{0:T(1024)(128)(4,1)}), s8[4194304]{0:T(1024)(128)(4,1)S(1)}, s32[]{:S(2)}) async-start(s8[5242880]{0:T(1024)(128)(4,1)} %bitcast.167), calls=%async_computation.2 | async-start | bytes 8388608
  46.1 9.6 %slice-start.1 = ((s8[5242880]{0:T(1024)(128)(4,1)}), s8[1048576]{0:T(1024)(128)(4,1)S(1)}, s32[]{:S(2)}) async-start(s8[5242880]{0:T(1024)(128)(4,1)} %bitcast.167), calls=%async_computation.3 | async-start | bytes 2097152
  46.1 1.8 %collective-permute-start.15 = (f32[512]{0:T(512)S(1)}, f32[512]{0:T(512)S(1)}, u32[]{:S(2)}, u32[]{:S(2)}) collective-permute-start(f32[512]{0:T(512)S(1)} %fusion), channel_id=1, source_target_pairs={{0,64},{64,0},{1,65},{65,1},{2,66},{66,2},{3,67},{67,3},{4,68},{68... | collective-permute-start | bytes 6152 | tf_op jit(solution)/shard_map/ppermute | solution.py:16
  47.9 7.8 %copy-start.4 = (f32[2048]{0:T(1024)S(1)}, f32[2048]{0:T(1024)}, u32[]{:S(2)}) copy-start(f32[2048]{0:T(1024)} %param.6) | copy-start | bytes 24580
  48.0 7.7 %collective-permute-start.16 = (f32[512]{0:T(512)S(1)}, f32[512]{0:T(512)S(1)}, u32[]{:S(2)}, u32[]{:S(2)}) collective-permute-start(f32[512]{0:T(512)S(1)} %add.259), channel_id=1, source_target_pairs={{0,128},{128,0},{1,129},{129,1},{2,130},{130,2},{3,131},{131,3},{4... | collective-permute-start | bytes 6152 | tf_op jit(solution)/shard_map/ppermute | solution.py:16
  54.2 4.7 %collective-permute-start.19 = (f16[2,128,1280]{2,1,0:T(8,128)(2,1)S(1)}, f16[2,128,1280]{2,1,0:T(8,128)(2,1)S(1)}, u32[]{:S(2)}, u32[]{:S(2)}) collective-permute-start(f16[2,128,1280]{2,1,0:T(8,128)(2,1)S(1)} %fusion.14), channel_id=1, source_target_pairs={{0,64},{64,0},{1,65},{65,1},{2,66},{66,2},{3,67},{67,3},{4,68},{68... | collective-permute-start | bytes 1966088 | tf_op jit(solution)/shard_map/ppermute | solution.py:16
  58.8 6.3 %collective-permute-start.17 = (f16[2,128,1280]{2,1,0:T(8,128)(2,1)S(1)}, f16[2,128,1280]{2,1,0:T(8,128)(2,1)S(1)}, u32[]{:S(2)}, u32[]{:S(2)}) collective-permute-start(f16[2,128,1280]{2,1,0:T(8,128)(2,1)S(1)} %fusion.13), channel_id=1, source_target_pairs={{0,64},{64,0},{1,65},{65,1},{2,66},{66,2},{3,67},{67,3},{4,68},{68... | collective-permute-start | bytes 1966088 | tf_op jit(solution)/shard_map/ppermute | solution.py:16
  59.1 6.3 %copy-start.1 = (f32[2,128,1280]{2,1,0:T(8,128)}, f32[2,128,1280]{2,1,0:T(8,128)S(1)}, u32[]{:S(2)}) copy-start(f32[2,128,1280]{2,1,0:T(8,128)S(1)} %bitcast_add_fusion) | copy-start | bytes 3932164
  59.1 24.8 %collective-permute-start.20 = (f16[128,1280]{1,0:T(8,128)(2,1)S(1)}, f16[128,1280]{1,0:T(8,128)(2,1)S(1)}, u32[]{:S(2)}, u32[]{:S(2)}) collective-permute-start(f16[128,1280]{1,0:T(8,128)(2,1)S(1)} %fusion.17), channel_id=1, source_target_pairs={{0,128},{128,0},{1,129},{129,1},{2,130},{130,2},{3,131},{131,3},{4... | collective-permute-start | bytes 983048 | tf_op jit(solution)/shard_map/ppermute | solution.py:16
  65.3 1.2 copy-start.3
  66.6 28.1 %collective-permute-start.18 = (f16[128,1280]{1,0:T(8,128)(2,1)}, f16[128,1280]{1,0:T(8,128)(2,1)S(1)}, u32[]{:S(2)}, u32[]{:S(2)}) collective-permute-start(f16[128,1280]{1,0:T(8,128)(2,1)} %fusion.16), channel_id=1, source_target_pairs={{0,128},{128,0},{1,129},{129,1},{2,130},{130,2},{3,131},{131,3},{4... | collective-permute-start | bytes 983048 | tf_op jit(solution)/shard_map/ppermute | solution.py:16
  68.3 27.6 %copy-start.2 = (f32[2,128,1280]{2,1,0:T(8,128)S(1)}, f32[2,128,1280]{2,1,0:T(8,128)}, u32[]{:S(2)}) copy-start(f32[2,128,1280]{2,1,0:T(8,128)} %copy-done.1) | copy-start | bytes 3932164
  119.6 5.7 %collective-permute-start.22 = (bf16[128,1280]{1,0:T(8,128)(2,1)S(1)}, bf16[128,1280]{1,0:T(8,128)(2,1)S(1)}, u32[]{:S(2)}, u32[]{:S(2)}) collective-permute-start(bf16[128,1280]{1,0:T(8,128)(2,1)S(1)} %subtract_convert_fusion), channel_id=1, source_target_pairs={{0,64},{64,0},{1,65},{65,1},{2,66},{66,2},{3,67},{67,3},{4,68},{68... | collective-permute-start | bytes 983048 | tf_op jit(solution)/shard_map/ppermute | solution.py:16
  119.7 21.1 %collective-permute-start.21 = (bf16[128,1280]{1,0:T(8,128)(2,1)S(1)}, bf16[128,1280]{1,0:T(8,128)(2,1)S(1)}, u32[]{:S(2)}, u32[]{:S(2)}) collective-permute-start(bf16[128,1280]{1,0:T(8,128)(2,1)S(1)} %subtract_convert_fusion), channel_id=1, source_target_pairs={{0,128},{128,0},{1,129},{129,1},{2,130},{130,2},{3,131},{131,3},{4... | collective-permute-start | bytes 983048 | tf_op jit(solution)/shard_map/ppermute | solution.py:16
  140.9 1.6 collective-permute-start.23
  162.8 3.8 %collective-permute-start.26 = (f16[8,896]{1,0:T(8,128)(2,1)S(1)}, f16[8,896]{1,0:T(8,128)(2,1)S(1)}, u32[]{:S(2)}, u32[]{:S(2)}) collective-permute-start(f16[8,896]{1,0:T(8,128)(2,1)S(1)} %get-tuple-element.26), channel_id=1, source_target_pairs={{0,12},{4,0},{8,4},{12,8},{1,13},{5,1},{9,5},{13,9},{2,14},{6,2},{... | collective-permute-start | bytes 43016 | tf_op jit(solution)/shard_map/ppermute | solution.py:16
  162.9 4.7 %collective-permute-start.25 = (f16[8,896]{1,0:T(8,128)(2,1)S(1)}, f16[8,896]{1,0:T(8,128)(2,1)S(1)}, u32[]{:S(2)}, u32[]{:S(2)}) collective-permute-start(f16[8,896]{1,0:T(8,128)(2,1)S(1)} %get-tuple-element.27), channel_id=1, source_target_pairs={{0,8},{4,12},{8,0},{12,4},{1,9},{5,13},{9,1},{13,5},{2,10},{6,14},... | collective-permute-start | bytes 43016 | tf_op jit(solution)/shard_map/ppermute | solution.py:16
  165.0 5.5 %collective-permute-start.24 = (f16[8,896]{1,0:T(8,128)(2,1)S(1)}, f16[8,896]{1,0:T(8,128)(2,1)S(1)}, u32[]{:S(2)}, u32[]{:S(2)}) collective-permute-start(f16[8,896]{1,0:T(8,128)(2,1)S(1)} %get-tuple-element.25), channel_id=1, source_target_pairs={{0,4},{4,8},{8,12},{12,0},{1,5},{5,9},{9,13},{13,1},{2,6},{6,10},{... | collective-permute-start | bytes 43016 | tf_op jit(solution)/shard_map/ppermute | solution.py:16
where the time goes:
time: 172 us; the launch traced here: 171 us
  waiting for transfers between devices  66.5 us (39%)
  starting transfers between devices  44.6 us (26%)
  blocking collectives  38.3 us (22%)
  other arithmetic  11.1 us (6%)
  matrix products  7.95 us (5%)
    ppermute x27, waiting for transfers between devices, shift(): lax.ppermute(value, axis, [(i, (i + distance) % n) for i in range(n)])  66.5 us
    ppermute x27, starting transfers between devices, shift(): lax.ppermute(value, axis, [(i, (i + distance) % n) for i in range(n)])  44.6 us
    all_to_all x1, blocking collectives, merge(): lax.all_to_all(jnp.tile(padded, (64, 1)), VOC, 0, 0, tiled=True)  19.8 us
    all_to_all x1, blocking collectives, scatter_grad(): lax.all_to_all(terms.reshape(16, 32, 896), ('x', 'y'), 0, 0, tiled=True)  18.5 us
    dot_general x2, matrix products, logits_of(): terms = jnp.dot(hidden, weight, preferred_element_type=jnp.float32)  4.52 us
  transfers between devices with their start and end apart: 27, of which 16 were waited for; matrix products, arithmetic and copies ran while one was open for 7% of the time, Pallas kernels for 0%

commit v1 on v0

--- a/solution.py
+++ b/solution.py
@@ -16,9 +16,9 @@
     return lax.ppermute(value, axis, [(i, (i + distance) % n) for i in range(n)])
 
 
-def gather4(value, axis, place):
+def gather4(value, axis, place, late=None):
     me = lax.axis_index(axis)
-    came = {d: shift(value, axis, d) for d in (2, 1, 3)}
+    came = {d: shift(value if d < 3 or late is None else late, axis, d) for d in (2, 1, 3)}
     blocks = [jnp.expand_dims(b, place) for b in (value, came[1], came[2], came[3])]
     shape = value.shape[:place] + (4,) + value.shape[place:]
     out = jnp.zeros(shape, value.dtype)
@@ -32,22 +32,27 @@
 def gather_hidden(value, cut):
     value = gather4(value, "zl", 0)
     first, second = value[..., :cut], value[..., cut:]
-    first = gather4(gather4(first, "y", 1), "x", 0)
-    second = gather4(gather4(second, "x", 0), "y", 2)
+    first = gather4(first, "y", 1)
+    second = gather4(second, "x", 0)
+    late, first = lax.optimization_barrier((second, first))
+    first, second = gather4(first, "x", 0), gather4(second, "y", 2, late)
     return first.reshape(512, -1), second.reshape(512, -1)
 
 
-def scatter_pair(value, axis):
+def trade_pair(value, axis):
     me = lax.axis_index(axis)
     give = lax.dynamic_index_in_dim(value, 1 - me, 0, keepdims=False).astype(jnp.float16)
-    keep = lax.dynamic_index_in_dim(value, me, 0, keepdims=False)
-    return keep + shift(give, axis, 1).astype(jnp.float32)
+    return lax.dynamic_index_in_dim(value, me, 0, keepdims=False), shift(give, axis, 1)
+
+
+def both_parts(kept, came):
+    return kept + came.astype(jnp.float32)
 
 
 def logits_of(hidden, weight):
     terms = jnp.dot(hidden, weight, preferred_element_type=jnp.float32)
     terms = terms.reshape(2, 2, 128, 1280).transpose(1, 0, 2, 3)
-    return scatter_pair(scatter_pair(terms, "c"), "zh")
+    return trade_pair(both_parts(*trade_pair(terms, "c")), "zh")
 
 
 def pick(value, index, dim):
@@ -101,25 +106,21 @@
     left = 2048 - cut
     wide = jnp.concatenate([first, second[:, :left]], axis=1).astype(jnp.float32)
     squares = jnp.sum(wide * wide, axis=1)
+    squares = squares + shift(squares, "zh", 1)
     squares = squares + shift(squares, "c", 1)
-    squares = squares + shift(squares, "zh", 1)
-    student = logits_of(second[:, left:], student_weight)
+    student = both_parts(*logits_of(second[:, left:], student_weight))
     inverse = lax.rsqrt(squares / D_T + EPS)
     normed = (wide * inverse[:, None] * norm_gain[None, :]).astype(jnp.bfloat16)
-    teacher = logits_of(normed, teacher_weight)
+    kept, came = logits_of(normed, teacher_weight)
 
+    s_top = jnp.max(student, axis=1)
+    s_total = jnp.sum(jnp.exp(student - s_top[:, None]), axis=1)
+    came, s_total = lax.optimization_barrier((came, s_total))
+    teacher = both_parts(kept, came)
     t_top = jnp.max(teacher, axis=1)
-    s_top = jnp.max(student, axis=1)
     t_exp = jnp.exp(teacher - t_top[:, None])
-    stats = jnp.stack(
-        [
-            t_top,
-            jnp.sum(t_exp, axis=1),
-            jnp.sum(t_exp * (teacher - student), axis=1),
-            s_top,
-            jnp.sum(jnp.exp(student - s_top[:, None]), axis=1),
-        ]
-    )
+    t_total, cross = jnp.sum(t_exp, axis=1), jnp.sum(t_exp * (teacher - student), axis=1)
+    stats = jnp.stack([t_top, t_total, cross, s_top, s_total])
     t_log, s_log, cross = merge(stats)
     kl_rows = cross - t_log + s_log
     grad = jnp.exp(student - s_log[:, None]) - jnp.exp(teacher - t_log[:, None])

time: 172 us -> 168 us (0.977)
  waiting for transfers between devices: 66.5 us -> 48.5 us
  starting transfers between devices: 44.6 us -> 53.3 us
  blocking collectives: 38.3 us -> 43.9 us
    ppermute x27, waiting for transfers between devices: 66.5 us -> 48.5 us  [shift(): lax.ppermute(value, axis, [(i, (i + distance) % n) for i in range(n)])]
    ppermute x27, starting transfers between devices: 44.6 us -> 53.3 us  [shift(): lax.ppermute(value, axis, [(i, (i + distance) % n) for i in range(n)])]
    all_to_all x1, blocking collectives: 19.8 us -> 24.1 us  [merge(): lax.all_to_all(jnp.tile(padded, (64, 1)), VOC, 0, 0, tiled=True)]
  transfers between devices with their start and end apart: 27 -> 27, of which waited for: 16 -> 14; matrix products, arithmetic and copies ran while one was open for 7% -> 8% of each run, Pallas kernels for 0% -> 0%
where the time goes in v1:
time: 168 us
  starting transfers between devices  53.3 us (32%)
  waiting for transfers between devices  48.5 us (29%)
  blocking collectives  43.9 us (26%)
  other arithmetic  11.3 us (7%)
  matrix products  7.95 us (5%)
    ppermute x27, starting transfers between devices, shift(): lax.ppermute(value, axis, [(i, (i + distance) % n) for i in range(n)])  53.3 us
    ppermute x27, waiting for transfers between devices, shift(): lax.ppermute(value, axis, [(i, (i + distance) % n) for i in range(n)])  48.5 us
    all_to_all x1, blocking collectives, merge(): lax.all_to_all(jnp.tile(padded, (64, 1)), VOC, 0, 0, tiled=True)  24.1 us
    all_to_all x1, blocking collectives, scatter_grad(): lax.all_to_all(terms.reshape(16, 32, 896), ('x', 'y'), 0, 0, tiled=True)  19.8 us
    dot_general x2, matrix products, logits_of(): terms = jnp.dot(hidden, weight, preferred_element_type=jnp.float32)  4.51 us
    dot_general x4, matrix products, terms(): lax.dot_general(grad, weight, (((1,), (1,)), ((), ())), preferred_element...  3.44 us
  transfers between devices with their start and end apart: 27, of which 14 were waited for; matrix products, arithmetic and copies ran while one was open for 8% of the time, Pallas kernels for 0%

profile of v1, /device:TPU:8, one launch (start us, length us, event | category | flops | bytes accessed | tf_op | source)
XLA Modules:
  0.0 167.5 jit_solution(66504436921187086)
XLA Ops:
  0.6 0.9 pad_add_fusion
  1.6 1.9 %collective-permute-start = (bf16[8,2944]{1,0:T(8,128)(2,1)S(1)}, bf16[8,2944]{1,0:T(8,128)(2,1)S(1)}, u32[]{:S(2)}, u32[]{:S(2)}) collective-permute-start(bf16[8,2944]{1,0:T(8,128)(2,1)S(1)} %pad_add_fusion), channel_id=1, source_target_pairs={{0,4},{4,8},{8,12},{12,0},{1,5},{5,9},{9,13},{13,1},{2,6},{6,10},{... | collective-permute-start | bytes 141320 | tf_op jit(solution)/shard_map/ppermute | solution.py:16
  3.5 3.3 %collective-permute-start.1 = (bf16[8,2944]{1,0:T(8,128)(2,1)S(1)}, bf16[8,2944]{1,0:T(8,128)(2,1)S(1)}, u32[]{:S(2)}, u32[]{:S(2)}) collective-permute-start(bf16[8,2944]{1,0:T(8,128)(2,1)S(1)} %pad_add_fusion), channel_id=1, source_target_pairs={{0,8},{4,12},{8,0},{12,4},{1,9},{5,13},{9,1},{13,5},{2,10},{6,14},... | collective-permute-start | bytes 141320 | tf_op jit(solution)/shard_map/ppermute | solution.py:16
  6.8 1.0 collective-permute-start.2
  7.8 0.8 bitcast_dynamic-update-slice_fusion.19
  8.6 1.7 collective-permute-done.1
  10.3 0.5 collective-permute-done.2
  10.9 1.6 collective-permute-start.3
  12.4 2.7 %collective-permute-start.4 = (bf16[4,8,1408]{2,1,0:T(8,128)(2,1)S(1)}, bf16[4,8,1408]{2,1,0:T(8,128)(2,1)S(1)}, u32[]{:S(2)}, u32[]{:S(2)}) collective-permute-start(bf16[4,8,1408]{2,1,0:T(8,128)(2,1)S(1)} %slice.38), channel_id=1, source_target_pairs={{0,32},{16,48},{32,0},{48,16},{1,33},{17,49},{33,1},{49,17},{2,34}... | collective-permute-start | bytes 270344 | tf_op jit(solution)/shard_map/ppermute | solution.py:16
  15.2 1.4 collective-permute-start.5
  16.6 1.6 collective-permute-start.6
  18.2 0.9 collective-permute-start.7
  19.3 2.5 %collective-permute-start.8 = (bf16[4,8,1536]{2,1,0:T(8,128)(2,1)S(1)}, bf16[4,8,1536]{2,1,0:T(8,128)(2,1)S(1)}, u32[]{:S(2)}, u32[]{:S(2)}) collective-permute-start(bf16[4,8,1536]{2,1,0:T(8,128)(2,1)S(1)} %slice.39), channel_id=1, source_target_pairs={{0,3},{1,0},{2,1},{3,2},{4,7},{5,4},{6,5},{7,6},{8,11},{9,8},{10,9... | collective-permute-start | bytes 294920 | tf_op jit(solution)/shard_map/ppermute | solution.py:16
  22.0 3.4 %collective-permute-start.13 = (bf16[4,4,8,1408]{3,2,1,0:T(8,128)(2,1)S(1)}, bf16[4,4,8,1408]{3,2,1,0:T(8,128)(2,1)S(1)}, u32[]{:S(2)}, u32[]{:S(2)}) collective-permute-start(bf16[4,4,8,1408]{3,2,1,0:T(8,128)(2,1)S(1)} %bitcast_dynamic-update-slice_fusion.12), channel_id=1, source_target_pairs={{0,2},{1,3},{2,0},{3,1},{4,6},{5,7},{6,4},{7,5},{8,10},{9,11},{10,... | collective-permute-start | bytes 1081352 | tf_op jit(solution)/shard_map/ppermute | solution.py:16
  25.4 0.1 broadcast_in_dim.106
  25.6 1.1 collective-permute-done.8
  26.7 0.7 collective-permute-start.9
  27.4 2.8 %collective-permute-start.11 = (bf16[4,4,8,1536]{3,2,1,0:T(8,128)(2,1)S(1)}, bf16[4,4,8,1536]{3,2,1,0:T(8,128)(2,1)S(1)}, u32[]{:S(2)}, u32[]{:S(2)}) collective-permute-start(bf16[4,4,8,1536]{3,2,1,0:T(8,128)(2,1)S(1)} %bitcast_dynamic-update-slice_fusion.11), channel_id=1, source_target_pairs={{0,48},{16,0},{32,16},{48,32},{1,49},{17,1},{33,17},{49,33},{2,50}... | collective-permute-start | bytes 1179656 | tf_op jit(solution)/shard_map/ppermute | solution.py:16
  30.1 0.1 broadcast_in_dim.86
  30.3 3.0 %collective-permute-done.12 = bf16[4,4,8,1408]{3,2,1,0:T(8,128)(2,1)S(1)} collective-permute-done((bf16[4,4,8,1408]{3,2,1,0:T(8,128)(2,1)S(1)}, bf16[4,4,8,1408]{3,2,1,0:T(8,128)(2,1)S(1)}, u32[]{:S(2)}, u32[]{:S(2)}) %collective-permute-start.12) | collective-permute-done | bytes 360480 | tf_op jit(solution)/shard_map/ppermute | solution.py:16
  33.3 7.5 %collective-permute-start.14 = (bf16[4,4,8,1408]{3,2,1,0:T(8,128)(2,1)S(1)}, bf16[4,4,8,1408]{3,2,1,0:T(8,128)(2,1)S(1)}, u32[]{:S(2)}, u32[]{:S(2)}) collective-permute-start(bf16[4,4,8,1408]{3,2,1,0:T(8,128)(2,1)S(1)} %bitcast_dynamic-update-slice_fusion.12), channel_id=1, source_target_pairs={{0,3},{1,0},{2,1},{3,2},{4,7},{5,4},{6,5},{7,6},{8,11},{9,8},{10,9... | collective-permute-start | bytes 1081352 | tf_op jit(solution)/shard_map/ppermute | solution.py:16
  40.9 4.9 %collective-permute-done.14 = bf16[4,4,8,1408]{3,2,1,0:T(8,128)(2,1)S(1)} collective-permute-done((bf16[4,4,8,1408]{3,2,1,0:T(8,128)(2,1)S(1)}, bf16[4,4,8,1408]{3,2,1,0:T(8,128)(2,1)S(1)}, u32[]{:S(2)}, u32[]{:S(2)}) %collective-permute-start.14) | collective-permute-done | bytes 360480 | tf_op jit(solution)/shard_map/ppermute | solution.py:16
  46.0 0.5 fusion
  46.5 5.4 %collective-permute-start.15 = (f32[512]{0:T(512)S(1)}, f32[512]{0:T(512)S(1)}, u32[]{:S(2)}, u32[]{:S(2)}) collective-permute-start(f32[512]{0:T(512)S(1)} %fusion), channel_id=1, source_target_pairs={{0,128},{128,0},{1,129},{129,1},{2,130},{130,2},{3,131},{131,3},{4... | collective-permute-start | bytes 6152 | tf_op jit(solution)/shard_map/ppermute | solution.py:16
  51.9 1.5 fusion.11
  53.5 0.8 collective-permute-done.15
  54.4 0.6 collective-permute-start.19
  54.9 0.5 collective-permute-done.16
  55.5 3.0 %fusion.3 = f32[512,1280]{1,0:T(8,128)S(1)} fusion(bf16[2048,1280]{1,0:T(8,128)(2,1)S(1)} %bitcast.168, f32[2048]{0:T(1024)S(1)} %copy-done.5, f32[512]{0:T(512)S(1)} %add_rsqrt_fusion, bf16[512,512]{1,0:T(8,128)(2,1)S(1)} %slice.40, bf16[512,1536]{1,0:T(8,128)(2,1)S(1)} %bitcast.142), kind=kOutput, calls=%fused_computation.5 | convolution fusion | flops 2691694592 | bytes 9971712 | tf_op jit(solution)/shard_map/dot_general | solution.py:53
  58.5 0.3 collective-permute-start.17
  58.8 0.1 bitcast_add_fusion
  59.0 5.2 %collective-permute-start.20 = (f16[128,1280]{1,0:T(8,128)(2,1)S(1)}, f16[128,1280]{1,0:T(8,128)(2,1)S(1)}, u32[]{:S(2)}, u32[]{:S(2)}) collective-permute-start(f16[128,1280]{1,0:T(8,128)(2,1)S(1)} %fusion.17), channel_id=1, source_target_pairs={{0,128},{128,0},{1,129},{129,1},{2,130},{130,2},{3,131},{131,3},{4... | collective-permute-start | bytes 983048 | tf_op jit(solution)/shard_map/ppermute | solution.py:16
  64.2 0.2 bitcast_add_fusion.1
  64.5 0.9 fusion.16
  65.3 0.3 copy-done.3
  65.6 1.6 collective-permute-start.18
  67.3 10.1 %collective-permute-done.20 = f16[128,1280]{1,0:T(8,128)(2,1)S(1)} collective-permute-done((f16[128,1280]{1,0:T(8,128)(2,1)S(1)}, f16[128,1280]{1,0:T(8,128)(2,1)S(1)}, u32[]{:S(2)}, u32[]{:S(2)}) %collective-permute-start.20) | collective-permute-done | bytes 327712 | tf_op jit(solution)/shard_map/ppermute | solution.py:16
  77.4 1.2 fusion.23
  78.6 1.3 exponential_reduce_fusion
  80.0 8.0 %collective-permute-done.18 = f16[128,1280]{1,0:T(8,128)(2,1)S(1)} collective-permute-done((f16[128,1280]{1,0:T(8,128)(2,1)}, f16[128,1280]{1,0:T(8,128)(2,1)S(1)}, u32[]{:S(2)}, u32[]{:S(2)}) %collective-permute-start.18) | collective-permute-done | bytes 327712 | tf_op jit(solution)/shard_map/ppermute | solution.py:16
  88.0 1.2 fusion.22
  89.2 0.3 multiply_reduce_fusion
  89.6 24.1 %all_to_all.11 = f32[64,8,128]{2,1,0:T(8,128)S(1)} all-to-all(f32[64,8,128]{2,1,0:T(8,128)S(1)} %tile.2), channel_id=1, replica_groups=mesh['zh'=2,'c'=2,'x'=4,'zl'=4,'y'=4] {'x','zl','y'}, dimensions={0} | all-to-all | bytes 524288 | tf_op jit(solution)/shard_map/all_to_all | solution.py:91
  113.7 0.1 fusion.24
  113.9 0.5 subtract_add_fusion
  114.4 1.6 subtract_convert_fusion
  116.1 5.2 %collective-permute-start.21 = (bf16[128,1280]{1,0:T(8,128)(2,1)S(1)}, bf16[128,1280]{1,0:T(8,128)(2,1)S(1)}, u32[]{:S(2)}, u32[]{:S(2)}) collective-permute-start(bf16[128,1280]{1,0:T(8,128)(2,1)S(1)} %subtract_convert_fusion), channel_id=1, source_target_pairs={{0,128},{128,0},{1,129},{129,1},{2,130},{130,2},{3,131},{131,3},{4... | collective-permute-start | bytes 983048 | tf_op jit(solution)/shard_map/ppermute | solution.py:16
  121.4 0.9 fusion.7
  122.2 0.9 fusion.8
  123.1 12.0 %collective-permute-done.21 = bf16[128,1280]{1,0:T(8,128)(2,1)S(1)} collective-permute-done((bf16[128,1280]{1,0:T(8,128)(2,1)S(1)}, bf16[128,1280]{1,0:T(8,128)(2,1)S(1)}, u32[]{:S(2)}, u32[]{:S(2)}) %collective-permute-start.21) | collective-permute-done | bytes 327712 | tf_op jit(solution)/shard_map/ppermute | solution.py:16
  135.1 0.9 fusion.9
  136.0 0.8 collective-permute-done.23
  136.7 0.8 fusion.10
  137.6 0.3 broadcast_select_fusion.7
  137.9 0.3 pad_maximum_fusion.2
  138.2 0.2 copy.50
  138.3 19.8 %all_to_all.12 = f16[16,32,896]{2,1,0:T(8,128)(2,1)S(1)} all-to-all(f16[16,32,896]{2,1,0:T(8,128)(2,1)S(1)} %bitcast.143), channel_id=1, replica_groups=mesh['zh'=2,'c'=2,'x'=4,'zl'=4,'y'=4] {'x','y'}, dimensions={0} | all-to-all | bytes 1835008 | tf_op jit(solution)/shard_map/all_to_all | solution.py:80
  158.2 0.1 convert_reduce_fusion
  158.5 3.0 %collective-permute-start.25 = (f16[8,896]{1,0:T(8,128)(2,1)S(1)}, f16[8,896]{1,0:T(8,128)(2,1)S(1)}, u32[]{:S(2)}, u32[]{:S(2)}) collective-permute-start(f16[8,896]{1,0:T(8,128)(2,1)S(1)} %get-tuple-element.34), channel_id=1, source_target_pairs={{0,8},{4,12},{8,0},{12,4},{1,9},{5,13},{9,1},{13,5},{2,10},{6,14},... | collective-permute-start | bytes 43016 | tf_op jit(solution)/shard_map/ppermute | solution.py:16
  161.4 0.3 collective-permute-start.24
  161.7 0.4 collective-permute-done.26
  162.2 1.1 collective-permute-done.25
  163.3 3.7 %collective-permute-done.24 = f16[8,896]{1,0:T(8,128)(2,1)S(1)} collective-permute-done((f16[8,896]{1,0:T(8,128)(2,1)S(1)}, f16[8,896]{1,0:T(8,128)(2,1)S(1)}, u32[]{:S(2)}, u32[]{:S(2)}) %collective-permute-start.24) | collective-permute-done | bytes 14368 | tf_op jit(solution)/shard_map/ppermute | solution.py:16
  166.9 0.6 fusion.20
  (73 shorter events, 1.3 us)
Async XLA Ops:
  0.6 51.3 %copy-start = (bf16[896,1280]{1,0:T(8,128)(2,1)S(1)}, bf16[896,1280]{1,0:T(8,128)(2,1)}, u32[]{:S(2)}) copy-start(bf16[896,1280]{1,0:T(8,128)(2,1)} %param.9) | copy-start | bytes 6881284
  1.6 7.0 %collective-permute-start = (bf16[8,2944]{1,0:T(8,128)(2,1)S(1)}, bf16[8,2944]{1,0:T(8,128)(2,1)S(1)}, u32[]{:S(2)}, u32[]{:S(2)}) collective-permute-start(bf16[8,2944]{1,0:T(8,128)(2,1)S(1)} %pad_add_fusion), channel_id=1, source_target_pairs={{0,4},{4,8},{8,12},{12,0},{1,5},{5,9},{9,13},{13,1},{2,6},{6,10},{... | collective-permute-start | bytes 141320 | tf_op jit(solution)/shard_map/ppermute | solution.py:16
  3.5 6.8 %collective-permute-start.1 = (bf16[8,2944]{1,0:T(8,128)(2,1)S(1)}, bf16[8,2944]{1,0:T(8,128)(2,1)S(1)}, u32[]{:S(2)}, u32[]{:S(2)}) collective-permute-start(bf16[8,2944]{1,0:T(8,128)(2,1)S(1)} %pad_add_fusion), channel_id=1, source_target_pairs={{0,8},{4,12},{8,0},{12,4},{1,9},{5,13},{9,1},{13,5},{2,10},{6,14},... | collective-permute-start | bytes 141320 | tf_op jit(solution)/shard_map/ppermute | solution.py:16
  6.8 4.1 %collective-permute-start.2 = (bf16[8,2944]{1,0:T(8,128)(2,1)S(1)}, bf16[8,2944]{1,0:T(8,128)(2,1)S(1)}, u32[]{:S(2)}, u32[]{:S(2)}) collective-permute-start(bf16[8,2944]{1,0:T(8,128)(2,1)S(1)} %pad_add_fusion), channel_id=1, source_target_pairs={{0,12},{4,0},{8,4},{12,8},{1,13},{5,1},{9,5},{13,9},{2,14},{6,2},{... | collective-permute-start | bytes 141320 | tf_op jit(solution)/shard_map/ppermute | solution.py:16
  10.9 8.4 %collective-permute-start.3 = (bf16[4,8,1408]{2,1,0:T(8,128)(2,1)S(1)}, bf16[4,8,1408]{2,1,0:T(8,128)(2,1)S(1)}, u32[]{:S(2)}, u32[]{:S(2)}) collective-permute-start(bf16[4,8,1408]{2,1,0:T(8,128)(2,1)S(1)} %slice.38), channel_id=1, source_target_pairs={{0,16},{16,32},{32,48},{48,0},{1,17},{17,33},{33,49},{49,1},{2,18}... | collective-permute-start | bytes 270344 | tf_op jit(solution)/shard_map/ppermute | solution.py:16
  12.4 9.4 %collective-permute-start.4 = (bf16[4,8,1408]{2,1,0:T(8,128)(2,1)S(1)}, bf16[4,8,1408]{2,1,0:T(8,128)(2,1)S(1)}, u32[]{:S(2)}, u32[]{:S(2)}) collective-permute-start(bf16[4,8,1408]{2,1,0:T(8,128)(2,1)S(1)} %slice.38), channel_id=1, source_target_pairs={{0,32},{16,48},{32,0},{48,16},{1,33},{17,49},{33,1},{49,17},{2,34}... | collective-permute-start | bytes 270344 | tf_op jit(solution)/shard_map/ppermute | solution.py:16
  15.2 6.7 %collective-permute-start.5 = (bf16[4,8,1408]{2,1,0:T(8,128)(2,1)S(1)}, bf16[4,8,1408]{2,1,0:T(8,128)(2,1)S(1)}, u32[]{:S(2)}, u32[]{:S(2)}) collective-permute-start(bf16[4,8,1408]{2,1,0:T(8,128)(2,1)S(1)} %slice.38), channel_id=1, source_target_pairs={{0,48},{16,0},{32,16},{48,32},{1,49},{17,1},{33,17},{49,33},{2,50}... | collective-permute-start | bytes 270344 | tf_op jit(solution)/shard_map/ppermute | solution.py:16
  16.6 9.0 %collective-permute-start.6 = (bf16[4,8,1536]{2,1,0:T(8,128)(2,1)S(1)}, bf16[4,8,1536]{2,1,0:T(8,128)(2,1)S(1)}, u32[]{:S(2)}, u32[]{:S(2)}) collective-permute-start(bf16[4,8,1536]{2,1,0:T(8,128)(2,1)S(1)} %slice.39), channel_id=1, source_target_pairs={{0,1},{1,2},{2,3},{3,0},{4,5},{5,6},{6,7},{7,4},{8,9},{9,10},{10,1... | collective-permute-start | bytes 294920 | tf_op jit(solution)/shard_map/ppermute | solution.py:16
  18.2 7.3 %collective-permute-start.7 = (bf16[4,8,1536]{2,1,0:T(8,128)(2,1)S(1)}, bf16[4,8,1536]{2,1,0:T(8,128)(2,1)S(1)}, u32[]{:S(2)}, u32[]{:S(2)}) collective-permute-start(bf16[4,8,1536]{2,1,0:T(8,128)(2,1)S(1)} %slice.39), channel_id=1, source_target_pairs={{0,2},{1,3},{2,0},{3,1},{4,6},{5,7},{6,4},{7,5},{8,10},{9,11},{10,... | collective-permute-start | bytes 294920 | tf_op jit(solution)/shard_map/ppermute | solution.py:16
  19.3 7.4 %collective-permute-start.8 = (bf16[4,8,1536]{2,1,0:T(8,128)(2,1)S(1)}, bf16[4,8,1536]{2,1,0:T(8,128)(2,1)S(1)}, u32[]{:S(2)}, u32[]{:S(2)}) collective-permute-start(bf16[4,8,1536]{2,1,0:T(8,128)(2,1)S(1)} %slice.39), channel_id=1, source_target_pairs={{0,3},{1,0},{2,1},{3,2},{4,7},{5,4},{6,5},{7,6},{8,11},{9,8},{10,9... | collective-permute-start | bytes 294920 | tf_op jit(solution)/shard_map/ppermute | solution.py:16
  21.9 11.4 %collective-permute-start.12 = (bf16[4,4,8,1408]{3,2,1,0:T(8,128)(2,1)S(1)}, bf16[4,4,8,1408]{3,2,1,0:T(8,128)(2,1)S(1)}, u32[]{:S(2)}, u32[]{:S(2)}) collective-permute-start(bf16[4,4,8,1408]{3,2,1,0:T(8,128)(2,1)S(1)} %bitcast_dynamic-update-slice_fusion.12), channel_id=1, source_target_pairs={{0,1},{1,2},{2,3},{3,0},{4,5},{5,6},{6,7},{7,4},{8,9},{9,10},{10,1... | collective-permute-start | bytes 1081352 | tf_op jit(solution)/shard_map/ppermute | solution.py:16
  22.0 18.9 %collective-permute-start.13 = (bf16[4,4,8,1408]{3,2,1,0:T(8,128)(2,1)S(1)}, bf16[4,4,8,1408]{3,2,1,0:T(8,128)(2,1)S(1)}, u32[]{:S(2)}, u32[]{:S(2)}) collective-permute-start(bf16[4,4,8,1408]{3,2,1,0:T(8,128)(2,1)S(1)} %bitcast_dynamic-update-slice_fusion.12), channel_id=1, source_target_pairs={{0,2},{1,3},{2,0},{3,1},{4,6},{5,7},{6,4},{7,5},{8,10},{9,11},{10,... | collective-permute-start | bytes 1081352 | tf_op jit(solution)/shard_map/ppermute | solution.py:16
  26.7 19.2 %collective-permute-start.9 = (bf16[4,4,8,1536]{3,2,1,0:T(8,128)(2,1)S(1)}, bf16[4,4,8,1536]{3,2,1,0:T(8,128)(2,1)S(1)}, u32[]{:S(2)}, u32[]{:S(2)}) collective-permute-start(bf16[4,4,8,1536]{3,2,1,0:T(8,128)(2,1)S(1)} %bitcast_dynamic-update-slice_fusion.11), channel_id=1, source_target_pairs={{0,16},{16,32},{32,48},{48,0},{1,17},{17,33},{33,49},{49,1},{2,18}... | collective-permute-start | bytes 1179656 | tf_op jit(solution)/shard_map/ppermute | solution.py:16
  27.4 18.5 %collective-permute-start.10 = (bf16[4,4,8,1536]{3,2,1,0:T(8,128)(2,1)S(1)}, bf16[4,4,8,1536]{3,2,1,0:T(8,128)(2,1)S(1)}, u32[]{:S(2)}, u32[]{:S(2)}) collective-permute-start(bf16[4,4,8,1536]{3,2,1,0:T(8,128)(2,1)S(1)} %bitcast_dynamic-update-slice_fusion.11), channel_id=1, source_target_pairs={{0,32},{16,48},{32,0},{48,16},{1,33},{17,49},{33,1},{49,17},{2,34}... | collective-permute-start | bytes 1179656 | tf_op jit(solution)/shard_map/ppermute | solution.py:16
  27.4 18.6 %collective-permute-start.11 = (bf16[4,4,8,1536]{3,2,1,0:T(8,128)(2,1)S(1)}, bf16[4,4,8,1536]{3,2,1,0:T(8,128)(2,1)S(1)}, u32[]{:S(2)}, u32[]{:S(2)}) collective-permute-start(bf16[4,4,8,1536]{3,2,1,0:T(8,128)(2,1)S(1)} %bitcast_dynamic-update-slice_fusion.11), channel_id=1, source_target_pairs={{0,48},{16,0},{32,16},{48,32},{1,49},{17,1},{33,17},{49,33},{2,50}... | collective-permute-start | bytes 1179656 | tf_op jit(solution)/shard_map/ppermute | solution.py:16
  33.3 12.5 %collective-permute-start.14 = (bf16[4,4,8,1408]{3,2,1,0:T(8,128)(2,1)S(1)}, bf16[4,4,8,1408]{3,2,1,0:T(8,128)(2,1)S(1)}, u32[]{:S(2)}, u32[]{:S(2)}) collective-permute-start(bf16[4,4,8,1408]{3,2,1,0:T(8,128)(2,1)S(1)} %bitcast_dynamic-update-slice_fusion.12), channel_id=1, source_target_pairs={{0,3},{1,0},{2,1},{3,2},{4,7},{5,4},{6,5},{7,6},{8,11},{9,8},{10,9... | collective-permute-start | bytes 1081352 | tf_op jit(solution)/shard_map/ppermute | solution.py:16
  46.0 9.4 %slice-start = ((s8[5242880]{0:T(1024)(128)(4,1)}), s8[4194304]{0:T(1024)(128)(4,1)S(1)}, s32[]{:S(2)}) async-start(s8[5242880]{0:T(1024)(128)(4,1)} %bitcast.167), calls=%async_computation.2 | async-start | bytes 8388608
  46.5 8.9 %slice-start.1 = ((s8[5242880]{0:T(1024)(128)(4,1)}), s8[1048576]{0:T(1024)(128)(4,1)S(1)}, s32[]{:S(2)}) async-start(s8[5242880]{0:T(1024)(128)(4,1)} %bitcast.167), calls=%async_computation.3 | async-start | bytes 2097152
  46.5 7.8 %collective-permute-start.15 = (f32[512]{0:T(512)S(1)}, f32[512]{0:T(512)S(1)}, u32[]{:S(2)}, u32[]{:S(2)}) collective-permute-start(f32[512]{0:T(512)S(1)} %fusion), channel_id=1, source_target_pairs={{0,128},{128,0},{1,129},{129,1},{2,130},{130,2},{3,131},{131,3},{4... | collective-permute-start | bytes 6152 | tf_op jit(solution)/shard_map/ppermute | solution.py:16
  53.5 2.0 %copy-start.5 = (f32[2048]{0:T(1024)S(1)}, f32[2048]{0:T(1024)}, u32[]{:S(2)}) copy-start(f32[2048]{0:T(1024)} %param.6) | copy-start | bytes 24580
  54.3 1.2 collective-permute-start.16
  54.4 4.5 %collective-permute-start.19 = (f16[2,128,1280]{2,1,0:T(8,128)(2,1)S(1)}, f16[2,128,1280]{2,1,0:T(8,128)(2,1)S(1)}, u32[]{:S(2)}, u32[]{:S(2)}) collective-permute-start(f16[2,128,1280]{2,1,0:T(8,128)(2,1)S(1)} %fusion.14), channel_id=1, source_target_pairs={{0,64},{64,0},{1,65},{65,1},{2,66},{66,2},{3,67},{67,3},{4,68},{68... | collective-permute-start | bytes 1966088 | tf_op jit(solution)/shard_map/ppermute | solution.py:16
  58.5 5.7 %collective-permute-start.17 = (f16[2,128,1280]{2,1,0:T(8,128)(2,1)S(1)}, f16[2,128,1280]{2,1,0:T(8,128)(2,1)S(1)}, u32[]{:S(2)}, u32[]{:S(2)}) collective-permute-start(f16[2,128,1280]{2,1,0:T(8,128)(2,1)S(1)} %fusion.13), channel_id=1, source_target_pairs={{0,64},{64,0},{1,65},{65,1},{2,66},{66,2},{3,67},{67,3},{4,68},{68... | collective-permute-start | bytes 1966088 | tf_op jit(solution)/shard_map/ppermute | solution.py:16
  58.9 5.5 %copy-start.1 = (f32[2,128,1280]{2,1,0:T(8,128)}, f32[2,128,1280]{2,1,0:T(8,128)S(1)}, u32[]{:S(2)}) copy-start(f32[2,128,1280]{2,1,0:T(8,128)S(1)} %bitcast_add_fusion) | copy-start | bytes 3932164
  59.0 18.4 %collective-permute-start.20 = (f16[128,1280]{1,0:T(8,128)(2,1)S(1)}, f16[128,1280]{1,0:T(8,128)(2,1)S(1)}, u32[]{:S(2)}, u32[]{:S(2)}) collective-permute-start(f16[128,1280]{1,0:T(8,128)(2,1)S(1)} %fusion.17), channel_id=1, source_target_pairs={{0,128},{128,0},{1,129},{129,1},{2,130},{130,2},{3,131},{131,3},{4... | collective-permute-start | bytes 983048 | tf_op jit(solution)/shard_map/ppermute | solution.py:16
  64.4 1.2 copy-start.3
  65.6 22.3 %collective-permute-start.18 = (f16[128,1280]{1,0:T(8,128)(2,1)}, f16[128,1280]{1,0:T(8,128)(2,1)S(1)}, u32[]{:S(2)}, u32[]{:S(2)}) collective-permute-start(f16[128,1280]{1,0:T(8,128)(2,1)} %fusion.16), channel_id=1, source_target_pairs={{0,128},{128,0},{1,129},{129,1},{2,130},{130,2},{3,131},{131,3},{4... | collective-permute-start | bytes 983048 | tf_op jit(solution)/shard_map/ppermute | solution.py:16
  67.3 21.9 %copy-start.2 = (f32[2,128,1280]{2,1,0:T(8,128)S(1)}, f32[2,128,1280]{2,1,0:T(8,128)}, u32[]{:S(2)}) copy-start(f32[2,128,1280]{2,1,0:T(8,128)} %copy-done.1) | copy-start | bytes 3932164
  67.3 21.9 %copy-start.4 = (f32[2,128,1280]{2,1,0:T(8,128)S(1)}, f32[2,128,1280]{2,1,0:T(8,128)}, u32[]{:S(2)}) copy-start(f32[2,128,1280]{2,1,0:T(8,128)} %copy-done.3) | copy-start | bytes 3932164
  116.0 6.2 %collective-permute-start.22 = (bf16[128,1280]{1,0:T(8,128)(2,1)S(1)}, bf16[128,1280]{1,0:T(8,128)(2,1)S(1)}, u32[]{:S(2)}, u32[]{:S(2)}) collective-permute-start(bf16[128,1280]{1,0:T(8,128)(2,1)S(1)} %subtract_convert_fusion), channel_id=1, source_target_pairs={{0,64},{64,0},{1,65},{65,1},{2,66},{66,2},{3,67},{67,3},{4,68},{68... | collective-permute-start | bytes 983048 | tf_op jit(solution)/shard_map/ppermute | solution.py:16
  116.1 19.0 %collective-permute-start.21 = (bf16[128,1280]{1,0:T(8,128)(2,1)S(1)}, bf16[128,1280]{1,0:T(8,128)(2,1)S(1)}, u32[]{:S(2)}, u32[]{:S(2)}) collective-permute-start(bf16[128,1280]{1,0:T(8,128)(2,1)S(1)} %subtract_convert_fusion), channel_id=1, source_target_pairs={{0,128},{128,0},{1,129},{129,1},{2,130},{130,2},{3,131},{131,3},{4... | collective-permute-start | bytes 983048 | tf_op jit(solution)/shard_map/ppermute | solution.py:16
  135.1 1.6 collective-permute-start.23
  158.4 3.8 %collective-permute-start.26 = (f16[8,896]{1,0:T(8,128)(2,1)S(1)}, f16[8,896]{1,0:T(8,128)(2,1)S(1)}, u32[]{:S(2)}, u32[]{:S(2)}) collective-permute-start(f16[8,896]{1,0:T(8,128)(2,1)S(1)} %get-tuple-element.33), channel_id=1, source_target_pairs={{0,12},{4,0},{8,4},{12,8},{1,13},{5,1},{9,5},{13,9},{2,14},{6,2},{... | collective-permute-start | bytes 43016 | tf_op jit(solution)/shard_map/ppermute | solution.py:16
  158.5 4.8 %collective-permute-start.25 = (f16[8,896]{1,0:T(8,128)(2,1)S(1)}, f16[8,896]{1,0:T(8,128)(2,1)S(1)}, u32[]{:S(2)}, u32[]{:S(2)}) collective-permute-start(f16[8,896]{1,0:T(8,128)(2,1)S(1)} %get-tuple-element.34), channel_id=1, source_target_pairs={{0,8},{4,12},{8,0},{12,4},{1,9},{5,13},{9,1},{13,5},{2,10},{6,14},... | collective-permute-start | bytes 43016 | tf_op jit(solution)/shard_map/ppermute | solution.py:16
  161.4 5.5 %collective-permute-start.24 = (f16[8,896]{1,0:T(8,128)(2,1)S(1)}, f16[8,896]{1,0:T(8,128)(2,1)S(1)}, u32[]{:S(2)}, u32[]{:S(2)}) collective-permute-start(f16[8,896]{1,0:T(8,128)(2,1)S(1)} %get-tuple-element.32), channel_id=1, source_target_pairs={{0,4},{4,8},{8,12},{12,0},{1,5},{5,9},{9,13},{13,1},{2,6},{6,10},{... | collective-permute-start | bytes 43016 | tf_op jit(solution)/shard_map/ppermute | solution.py:16
